TPU v7x, 32 devices: a whole 2x2x4 slice. The times are simulated.
32 devices in a mesh: groups: 2 (over y), seq: 4 (over z), tensor: 4 (over x, core).
Axes of the slice: x: 2, y: 2, z: 4, core: 2. Of those that a mesh axis runs over, the one named last changes fastest.
Arguments:
- text_states: bfloat16 [64, 8192], P(('groups', 'seq')), parts along dimension 0, may hold values from -18 to 18
- vision_states: bfloat16 [2048, 8192], P(('groups', 'seq'), 'tensor'), parts along dimension 0, may hold values from -6 to 6
- norm_gain: bfloat16 [8192], replicated, may hold values from 0.25 to 1.75
- query_weight: bfloat16 [8192, 8192], P('seq', 'tensor'), may hold values from -0.0625 to 0.0625
- key_value_weight: bfloat16 [2, 8192, 1024], P(None, 'tensor', 'seq'), may hold values from -0.0625 to 0.0625
- out_weight: bfloat16 [8192, 8192], P('tensor', 'seq'), may hold values from -0.0625 to 0.0625
- query_gain: float32 [128], replicated, may hold values from 4.5 to 6
- key_norm_gain: float32 [128], replicated, may hold values from 4.5 to 6
- attn_gate: float32 [1], replicated, may hold values from 0.4 to 2
- tile_counts: int32 [4], P('groups'), parts along dimension 0, may hold values from 128 to 512, as said below
- tile_mask: int32 [2, 2], P('groups'), parts along dimension 0, may hold values from 0 to 1, as said below
Outputs:
- layer_out: bfloat16 [64, 8192], P(('groups', 'tensor'), 'seq'), parts along dimension 0
There are 2 independent parts, one for each index of `groups`. A program takes and returns all parts, laid end to end along the dimension named above; an argument that names none is the same for every part. Nothing has to cross between parts.
Inputs may be any that keep to these rules, and one draw needn't show every extreme that they name: `tile_counts`: some tile is full (512 valid tokens) and some tile holds exactly 128; valid tokens are the first slots of a tile. `tile_mask`: every row has at least one 1 and at least one 0.
All inputs are finite; a program needn't handle non-finite values.
Results may differ from a plain program's by a relative error of at most 0.0055.
The roundings to bfloat16 on the way count: a program that leaves them out, or rounds other values in their place, can miss the bound.
Values may be sent and summed in bfloat16 or wider, within the bound.
A program may use at most 128 MiB of HBM per device.

v0:
```python
import jax
import jax.numpy as jnp
from jax import lax
from jax.sharding import PartitionSpec as P

TILE_LEN = 512
TEXT_BLOCK = 32
EPS = 1e-05
NEG = -1e30


def combined_all(part, axis, combine):
    gathered = jax.tree.map(lambda a: lax.all_gather(a, axis), part)

    def take(source):
        return jax.tree.map(lambda a: lax.dynamic_index_in_dim(a, source, 0, False), gathered)

    return lax.fori_loop(
        1, lax.axis_size(axis), lambda source, state: combine(state, take(source)), take(0)
    )


def root_mean_rows(value_matrix, gain):
    mean_sq = jnp.mean(value_matrix * value_matrix, axis=-1, keepdims=True)
    return value_matrix * lax.rsqrt(mean_sq + EPS) * gain


def allowed_mask(query_count, key_start, key_count, tile_counts, tile_mask):
    tiles = tile_counts.shape[0]
    blocks = tile_mask.shape[0]
    key_pos = key_start + jnp.arange(key_count, dtype=jnp.int32)
    key_tile = key_pos // TILE_LEN
    tile_match = key_tile[:, None] == jnp.arange(tiles, dtype=jnp.int32)[None, :]
    count_here = jnp.sum(jnp.where(tile_match, tile_counts[None, :], 0), axis=1)
    slot_ok = key_pos % TILE_LEN < count_here
    query_pos = jnp.arange(query_count, dtype=jnp.int32)
    block_match = (
        query_pos[:, None] // TEXT_BLOCK == jnp.arange(blocks, dtype=jnp.int32)[None, :]
    ).astype(jnp.float32)
    row_tiles = jnp.dot(block_match, tile_mask.astype(jnp.float32), precision=lax.Precision.HIGHEST)
    seen = jnp.dot(row_tiles, tile_match.astype(jnp.float32).T, precision=lax.Precision.HIGHEST)
    return (seen > 0.5) & slot_ok[None, :]


def partial_attend(query_matrix, key_matrix, value_matrix, allowed):
    scale = query_matrix.shape[-1] ** (-0.5)
    scores = (
        jnp.einsum("ihgd,khd->ihgk", query_matrix, key_matrix, preferred_element_type=jnp.float32)
        * scale
    )
    mask = allowed[:, None, None, :]
    masked = jnp.where(mask, scores, NEG)
    top = jnp.max(masked, axis=-1)
    weights = jnp.where(mask, jnp.exp(masked - top[..., None]), 0.0)
    total = jnp.sum(weights, axis=-1)
    summed = jnp.einsum("ihgk,khd->ihgd", weights, value_matrix, precision=lax.Precision.HIGHEST)
    return (top, total, summed)


def join_parts(first, second):
    top = jnp.maximum(first[0], second[0])
    scale_first = jnp.exp(first[0] - top)
    scale_second = jnp.exp(second[0] - top)
    total = first[1] * scale_first + second[1] * scale_second
    summed = first[2] * scale_first[..., None] + second[2] * scale_second[..., None]
    return (top, total, summed)


def local(
    text_states,
    vision_states,
    norm_gain,
    query_weight,
    key_value_weight,
    out_weight,
    query_gain,
    key_norm_gain,
    attn_gate,
    tile_counts,
    tile_mask,
):
    seq_count = lax.axis_size("seq")
    seq_index = lax.axis_index("seq")
    tensor_count = lax.axis_size("tensor")
    tensor_index = lax.axis_index("tensor")
    text_dev = text_states.shape[0]
    text_all = text_dev * seq_count
    vis_dev = vision_states.shape[0]
    head_size = query_gain.shape[0]
    query_local = query_weight.shape[1] // head_size
    normed = root_mean_rows(text_states.astype(jnp.float32), norm_gain.astype(jnp.float32)).astype(
        jnp.bfloat16
    )
    raw_cols, normed_cols = (
        lax.all_to_all(text_states, "seq", split_axis=1, concat_axis=0, tiled=True),
        lax.all_to_all(normed, "seq", split_axis=1, concat_axis=0, tiled=True),
    )
    rows = normed_cols
    query_raw = lax.psum_scatter(
        jnp.dot(rows, query_weight, preferred_element_type=jnp.float32),
        "seq",
        scatter_dimension=0,
        tiled=True,
    )
    query_matrix = root_mean_rows(
        query_raw.reshape(text_dev, query_local, head_size), query_gain
    ).astype(jnp.bfloat16)
    kv_full = jnp.einsum(
        "vd,jdc->jvc",
        vision_states,
        lax.all_gather(key_value_weight, "seq", axis=2, tiled=True),
        preferred_element_type=jnp.float32,
    )
    kv_local = lax.psum_scatter(kv_full, "tensor", scatter_dimension=2, tiled=True)
    kv_heads = kv_local.shape[2] // head_size
    group_size = query_local // kv_heads
    key_matrix = root_mean_rows(
        kv_local[0].reshape(vis_dev, kv_heads, head_size), key_norm_gain
    ).astype(jnp.bfloat16)
    value_matrix = kv_local[1].astype(jnp.bfloat16).reshape(vis_dev, kv_heads, head_size)
    queries_grouped = query_matrix.reshape(text_dev, kv_heads, group_size, head_size)
    query_all = lax.all_gather(queries_grouped, "seq", axis=0, tiled=True)
    allowed = allowed_mask(text_all, seq_index * vis_dev, vis_dev, tile_counts, tile_mask)
    local_parts = partial_attend(query_all, key_matrix, value_matrix.astype(jnp.float32), allowed)
    top, total, summed = combined_all(local_parts, "seq", join_parts)
    attention_all = (
        (summed / total[..., None]).reshape(text_all, query_local * head_size).astype(jnp.bfloat16)
    )
    rows_out = text_all // tensor_count
    rows = attention_all
    branch = lax.psum_scatter(
        jnp.dot(rows, out_weight, preferred_element_type=jnp.float32),
        "tensor",
        scatter_dimension=0,
        tiled=True,
    )
    residual = lax.dynamic_slice_in_dim(raw_cols, tensor_index * rows_out, rows_out, 0)
    return (residual.astype(jnp.float32) + jnp.tanh(attn_gate[0]) * branch).astype(jnp.bfloat16)


def solution(mesh):
    return jax.shard_map(
        local,
        mesh=mesh,
        in_specs=(
            P(("groups", "seq"), None),
            P(("groups", "seq"), "tensor"),
            P(),
            P("seq", "tensor"),
            P(None, "tensor", "seq"),
            P("tensor", "seq"),
            P(),
            P(),
            P(),
            P("groups"),
            P("groups", None),
        ),
        out_specs=P(("groups", "tensor"), "seq"),
        check_vma=False,
    )
```

profile of v0, /device:TPU:0, one launch (start us, length us, event | category | flops | bytes accessed | tf_op | source)
XLA Modules:
  0.0 289.4 jit_solution(2777696798040319785)
XLA Ops:
  6.5 4.1 %copy.87 = bf16[2,2048,256]{1,2,0:T(8,128)(2,1)} copy(bf16[2,2048,256]{2,1,0:T(8,128)(2,1)} %param.17) | data formatting | bytes 4194304 | tf_op args[4]
  10.6 0.0 all-gather.6.cloned.1.call-update
  10.7 0.0 reduce-scatter.6.cloned.1.call-start
  10.7 0.7 convert_element_type.43
  11.4 1.1 fusion.9
  12.5 1.0 fusion.11
  13.5 12.2 %all_to_all.38 = bf16[8,4,2048]{2,0,1:T(8,128)(2,1)S(1)} all-to-all(bf16[8,4,2048]{2,0,1:T(8,128)(2,1)S(1)} %bitcast.84), channel_id=1, replica_groups=mesh['groups'=2,'seq'=4,'tensor'=4] {'seq'}, dimensions={1} | all-to-all | bytes 262144 | tf_op jit(solution)/shard_map/all_to_all | solution.py:96
  25.7 5.9 %fusion.20 = f32[32,2048]{1,0:T(8,128)} fusion(bf16[2048,2048]{1,0:T(8,128)(2,1)} %param.16, bf16[8,4,2048]{2,0,1:T(8,128)(2,1)S(1)} %all_to_all.38), kind=kOutput, calls=%fused_computation.36 | convolution fusion | flops 268435456 | bytes 8781824 | tf_op jit(solution)/shard_map/dot_general | solution.py:100
  31.6 0.0 reduce-scatter.6.cloned.1.call-update
  31.7 0.0 copy-start.1
  31.7 0.0 reduce-scatter.4.cloned.1.call-start
  31.8 131.4 %all-gather.6.cloned.1.call-done = bf16[2,2048,1024]{1,2,0:T(8,128)(2,1)} async-done(((bf16[2,2048,256]{1,2,0:T(8,128)(2,1)}), bf16[2,2048,1024]{1,2,0:T(8,128)(2,1)}) %all-gather.6.cloned.1.call-update) | async-done | bytes 8388624 | tf_op jit(solution)/shard_map/all_gather | solution.py:111
  163.2 7.2 %convolution_bitcast_fusion = f32[2,256,1024]{1,2,0:T(8,128)} fusion(bf16[2,2048,1024]{1,2,0:T(8,128)(2,1)} %all-gather.6.cloned.1.call-done, bf16[256,2048]{1,0:T(8,128)(2,1)S(1)} %copy-done), kind=kOutput, calls=%fused_computation.10 | convolution fusion | flops 2147483648 | bytes 11534336 | tf_op jit(solution)/shard_map/vd,jdc->jvc/dot_general | solution.py:108
  170.3 0.0 reduce-scatter.4.cloned.1.call-update
  170.3 0.0 all-gather.8.cloned.1.call-start
  170.4 0.1 select_reduce_fusion
  170.5 0.2 fusion.6
  170.8 12.5 %reduce-scatter.6.cloned.1.call-done = f32[8,2048]{1,0:T(8,128)} async-done(((f32[32,2048]{1,0:T(8,128)}), f32[8,2048]{1,0:T(8,128)}) %reduce-scatter.6.cloned.1.call-update) | async-done | bytes 65552 | tf_op jit(solution)/shard_map/reduce_scatter | solution.py:99
  183.3 0.9 bitcast_reduce_fusion
  184.2 0.1 copy.89
  184.3 0.1 copy.105
  184.4 0.9 multiply_convert_fusion.1
  185.3 12.3 %all_gather.25 = bf16[32,2,8,128]{3,0,2,1:T(8,128)(2,1)S(1)} all-gather(bf16[8,2,8,128]{3,0,2,1:T(8,128)(2,1)S(1)} %multiply_convert_fusion.1), channel_id=1, replica_groups=mesh['groups'=2,'seq'=4,'tensor'=4] {'seq'}, dimensions={0}, use_global_device_ids=true | all-gather | bytes 163840 | tf_op jit(solution)/shard_map/all_gather | solution.py:122
  197.6 18.1 %reduce-scatter.4.cloned.1.call-done = f32[2,256,256]{1,2,0:T(8,128)} async-done(((f32[2,256,1024]{1,2,0:T(8,128)}), f32[2,256,256]{1,2,0:T(8,128)}) %reduce-scatter.4.cloned.1.call-update) | async-done | bytes 524304 | tf_op jit(solution)/shard_map/reduce_scatter | solution.py:114
  215.7 1.0 slice.15
  216.6 0.1 copy.88
  216.8 0.4 fusion.33
  217.2 1.0 slice.21
  218.2 1.2 convolution_bitcast_fusion.1
  219.4 0.0 all-gather.8.cloned.1.call-update
  219.4 0.0 reduce-scatter.8.cloned.1.call-start
  219.5 0.1 copy.91
  219.6 0.3 fusion.8
  219.9 0.1 copy.92
  219.9 13.8 %all-gather.1 = f32[128,2,8]{2,1,0:T(2,128)S(1)} all-gather(f32[32,2,8]{2,1,0:T(2,128)S(1)} %copy.92), channel_id=3, replica_groups=mesh['groups'=2,'seq'=4,'tensor'=4] {'seq'}, dimensions={0}, use_global_device_ids=true | all-gather | bytes 10240 | tf_op jit(solution)/shard_map/all_gather | solution.py:13
  233.7 0.1 copy.97
  233.8 0.1 copy.100
  233.9 14.5 %all-gather = f32[128,2,8]{2,1,0:T(2,128)S(1)} all-gather(f32[32,2,8]{2,1,0:T(2,128)S(1)} %copy.91), channel_id=2, replica_groups=mesh['groups'=2,'seq'=4,'tensor'=4] {'seq'}, dimensions={0}, use_global_device_ids=true | all-gather | bytes 10240 | tf_op jit(solution)/shard_map/all_gather | solution.py:13
  248.3 0.1 copy.96
  248.4 0.1 copy.99
  248.5 2.2 all-gather.8.cloned.1.call-done
  250.7 1.0 slice.19
  251.7 0.2 copy.98
  251.9 4.5 %while.19 = (s32[]{:T(128)}, f32[32,2,8]{0,2,1:T(8,128)S(1)}, f32[32,2,8]{0,2,1:T(8,128)S(1)}, f32[32,2,8,128]{3,2,1,0:T(8,128)S(1)}, f32[4,32,2,8]{1,3,2,0:T(8,...) while((s32[]{:T(128)}, f32[32,2,8]{0,2,1:T(8,128)S(1)}, ...), condition=%wide.region_9.10_spmd, body=%wide.region_8.9_spmd.sunk | while | flops 199685 | bytes 1339543 | solution.py:18
  251.9 0.1 copy.127
  252.0 0.1 copy.128
  252.1 1.0 constant_dynamic-slice_fusion.2
  253.1 0.3 fusion.42
  253.4 0.1 copy.127
  253.5 0.1 copy.128
  253.6 1.0 constant_dynamic-slice_fusion.2
  254.6 0.3 fusion.42
  254.9 0.1 copy.127
  255.0 0.1 copy.128
  255.1 1.0 constant_dynamic-slice_fusion.2
  256.1 0.3 fusion.42
  256.4 0.1 copy.102
  256.5 0.1 divide_convert_fusion
  256.6 5.6 %fusion.17 = f32[32,2048]{1,0:T(8,128)} fusion(bf16[2048,2048]{1,0:T(8,128)(2,1)} %param.18, bf16[4,8,16,128]{3,2,1,0:T(8,128)(2,1)S(1)} %bitcast.80), kind=kOutput, calls=%fused_computation.33 | convolution fusion | flops 268435456 | bytes 8781824 | tf_op jit(solution)/shard_map/dot_general | solution.py:132
  262.3 0.0 reduce-scatter.8.cloned.1.call-update
  262.3 3.3 %all-to-all-start = ((bf16[8,4,2048]{2,0,1:T(8,128)(2,1)}), bf16[8,4,2048]{2,0,1:T(8,128)(2,1)S(1)}, u32[]{:S(2)}, u32[]{:S(2)}) async-start(bf16[8,4,2048]{2,0,1:T(8,128)(2,1)} %bitcast.3), calls=%async_computation | async-start | bytes 262144 | tf_op jit(solution)/shard_map/all_to_all | solution.py:95
  266.3 5.5 %all-to-all-done = bf16[8,4,2048]{2,0,1:T(8,128)(2,1)S(1)} async-done(((bf16[8,4,2048]{2,0,1:T(8,128)(2,1)}), bf16[8,4,2048]{2,0,1:T(8,128)(2,1)S(1)}, u32[]{:S(2)}, u32[]{:S(2)}) %all-to-all-start) | async-done | bytes 131104 | tf_op jit(solution)/shard_map/all_to_all | solution.py:95
  271.9 9.6 %reduce-scatter.8.cloned.1.call-done = f32[8,2048]{1,0:T(8,128)} async-done(((f32[32,2048]{1,0:T(8,128)}), f32[8,2048]{1,0:T(8,128)}) %reduce-scatter.8.cloned.1.call-update) | async-done | bytes 65552 | tf_op jit(solution)/shard_map/reduce_scatter | solution.py:131
  281.4 1.5 add_convert_fusion
  (23 shorter events, 0.2 us)
Async XLA Ops:
  6.5 156.6 %copy-start = (bf16[256,2048]{1,0:T(8,128)(2,1)S(1)}, bf16[256,2048]{1,0:T(8,128)(2,1)}, u32[]{:S(2)}) copy-start(bf16[256,2048]{1,0:T(8,128)(2,1)} %param.14) | copy-start | bytes 3145732
  6.5 156.6 %all-gather.6.cloned.1.call-start = ((), (), s32[]{:S(2)}) async-start(), calls=%async_computation.5 | async-start | bytes 10485760 | tf_op jit(solution)/shard_map/all_gather | solution.py:111
  10.7 172.6 %reduce-scatter.6.cloned.1.call-start = ((), (), s32[]{:S(2)}) async-start(), calls=%async_computation.7 | async-start | bytes 327680 | tf_op jit(solution)/shard_map/reduce_scatter | solution.py:99
  31.7 138.8 %copy-start.3 = (s32[2]{0:T(128)S(1)}, s32[2]{0:T(128)}, u32[]{:S(2)}) copy-start(s32[2]{0:T(128)} %param.22) | copy-start | bytes 28
  31.7 138.9 %copy-start.4 = (s32[1,2]{1,0:T(1,128)S(1)}, s32[1,2]{1,0:T(1,128)}, u32[]{:S(2)}) copy-start(s32[1,2]{1,0:T(1,128)} %param.23) | copy-start | bytes 28
  31.7 152.7 %copy-start.1 = (f32[128]{0:T(128)S(1)}, f32[128]{0:T(128)}, u32[]{:S(2)}) copy-start(f32[128]{0:T(128)} %param.19) | copy-start | bytes 1540
  31.7 185.1 %copy-start.2 = (f32[128]{0:T(128)S(1)}, f32[128]{0:T(128)}, u32[]{:S(2)}) copy-start(f32[128]{0:T(128)} %param.20) | copy-start | bytes 1540
  31.7 184.0 %reduce-scatter.4.cloned.1.call-start = ((), (), s32[]{:S(2)}) async-start(), calls=%async_computation.6 | async-start | bytes 2621440 | tf_op jit(solution)/shard_map/reduce_scatter | solution.py:114
  170.3 80.4 %all-gather.8.cloned.1.call-start = ((), (), s32[]{:S(2)}) async-start(), calls=%async_computation.9 | async-start | bytes 1310720 | tf_op jit(solution)/shard_map/all_gather | solution.py:13
  219.4 62.0 %reduce-scatter.8.cloned.1.call-start = ((), (), s32[]{:S(2)}) async-start(), calls=%async_computation.8 | async-start | bytes 327680 | tf_op jit(solution)/shard_map/reduce_scatter | solution.py:131
  262.3 9.6 %all-to-all-start = ((bf16[8,4,2048]{2,0,1:T(8,128)(2,1)}), bf16[8,4,2048]{2,0,1:T(8,128)(2,1)S(1)}, u32[]{:S(2)}, u32[]{:S(2)}) async-start(bf16[8,4,2048]{2,0,1:T(8,128)(2,1)} %bitcast.3), calls=%async_computation | async-start | bytes 262144 | tf_op jit(solution)/shard_map/all_to_all | solution.py:95
Sparse Core Ops, SparseCore 0:
  10.8 152.3 all-gather.5
  165.4 17.8 reduce-scatter.5
  186.0 29.6 reduce-scatter.3
  219.6 31.1 all-gather.7
  262.4 18.9 reduce-scatter.7
where the time goes:
time: 290 us; the launch traced here: 289 us
  waiting for transfers between devices  179 us (62%)
  blocking collectives  52.7 us (18%)
  matrix products  20.5 us (7%)
  between operations  14 us (5%)
  local copies, waits for them, and re-layouts  11.5 us (4%)
  other arithmetic  7.69 us (3%)
  starting transfers between devices  3.51 us (1%)
    all_gather x1, waiting for transfers between devices, local(): lax.all_gather(key_value_weight, 'seq', axis=2, tiled=True)  131 us
    all_gather x2, blocking collectives, combined_all(): gathered = jax.tree.map(lambda a: lax.all_gather(a, axis), part)  28.2 us
    reduce_scatter x1, waiting for transfers between devices, local(): lax.psum_scatter(kv_full, 'tensor', scatter_dimension=2, tiled=True)  18.1 us
    reduce_scatter x1, waiting for transfers between devices, local(): lax.psum_scatter(jnp.dot(rows, query_weight, preferred_element_type=jnp.f...  12.5 us
    all_gather x1, blocking collectives, local(): query_all = lax.all_gather(queries_grouped, 'seq', axis=0, tiled=True)  12.3 us
    all_to_all x1, blocking collectives, local(): lax.all_to_all(normed, 'seq', split_axis=1, concat_axis=0, tiled=True)  12.2 us
    reduce_scatter x1, waiting for transfers between devices, local(): lax.psum_scatter(jnp.dot(rows, out_weight, preferred_element_type=jnp.flo...  9.56 us
    dot_general x1, matrix products, local(): jnp.einsum('vd,jdc->jvc', vision_states, lax.all_gather(key_value_weight,...  7.17 us
  transfers between devices with their start and end apart: 6, of which 6 were waited for; matrix products, arithmetic and copies ran while one was open for 7% of the time, Pallas kernels for 0%

commit v1 on v0

--- a/solution.py
+++ b/solution.py
@@ -7,6 +7,24 @@
 TEXT_BLOCK = 32
 EPS = 1e-05
 NEG = -1e30
+
+
+def gather_around(array, axis, dim):
+    ways, here, lap = (lax.axis_size(axis), lax.axis_index(axis), array.shape[dim])
+    lengths = [n * ways if d == dim else n for d, n in enumerate(array.shape)]
+    full = lax.dynamic_update_slice_in_dim(
+        jnp.zeros(lengths, array.dtype), array, here * lap, axis=dim
+    )
+    going_up = going_down = array
+    for far in range(1, ways // 2 + 1):
+        going_up = lax.ppermute(going_up, axis, [(d, (d + 1) % ways) for d in range(ways)])
+        full = lax.dynamic_update_slice_in_dim(full, going_up, (here - far) % ways * lap, axis=dim)
+        if 2 * far < ways:
+            going_down = lax.ppermute(going_down, axis, [(d, (d - 1) % ways) for d in range(ways)])
+            full = lax.dynamic_update_slice_in_dim(
+                full, going_down, (here + far) % ways * lap, axis=dim
+            )
+    return full
 
 
 def combined_all(part, axis, combine):
@@ -108,7 +126,7 @@
     kv_full = jnp.einsum(
         "vd,jdc->jvc",
         vision_states,
-        lax.all_gather(key_value_weight, "seq", axis=2, tiled=True),
+        gather_around(key_value_weight, "seq", 2),
         preferred_element_type=jnp.float32,
     )
     kv_local = lax.psum_scatter(kv_full, "tensor", scatter_dimension=2, tiled=True)

time: 290 us -> 285 us (0.983)
  waiting for transfers between devices: 179 us -> 113 us
  starting transfers between devices: 3.51 us -> 55.2 us
  local copies, waits for them, and re-layouts: 11.5 us -> 31.9 us
  blocking collectives: 52.7 us -> 40.5 us
    all_gather x1 -> x0, waiting for transfers between devices: 131 us -> none  [local(): lax.all_gather(key_value_weight, 'seq', axis=2, tiled=True)]
    all_to_all x0 -> x1, starting transfers between devices: none -> 46.7 us  [local(): lax.all_to_all(normed, 'seq', split_axis=1, concat_axis=0, tiled=True)]
    ppermute x0 -> x3, waiting for transfers between devices: none -> 45 us  [the longest x2 45 us: gather_around(): lax.ppermute(going_up, axis, [(d, (d + 1) % ways) for d in range(ways)])]
    all_to_all x0 -> x1, waiting for transfers between devices: none -> 34.7 us  [local(): lax.all_to_all(normed, 'seq', split_axis=1, concat_axis=0, tiled=True)]
    reduce_scatter x1, waiting for transfers between devices: 12.5 us -> 0.02 us  [local(): lax.psum_scatter(jnp.dot(rows, query_weight, preferred_element_type=jnp.f...]
    all_to_all x1 -> x0, blocking collectives: 12.2 us -> none  [local(): lax.all_to_all(normed, 'seq', split_axis=1, concat_axis=0, tiled=True)]
    ppermute x0 -> x3, local copies, waits for them, and re-layouts: none -> 9.87 us  [the longest x2 5.88 us: gather_around(): lax.ppermute(going_up, axis, [(d, (d + 1) % ways) for d in range(ways)])]
    dynamic_update_slice x0 -> x4, local copies, waits for them, and re-layouts: none -> 7.48 us  [the longest x1 3.16 us: gather_around(): lax.dynamic_update_slice_in_dim(full, going_down, (here + far) % ways * l...]
  transfers between devices with their start and end apart: 6 -> 9, of which waited for: 6 -> 6; matrix products, arithmetic and copies ran while one was open for 7% -> 16% of each run, Pallas kernels for 0% -> 0%
where the time goes in v1:
time: 285 us; the launch traced here: 284 us
  waiting for transfers between devices  113 us (40%)
  starting transfers between devices  55.2 us (19%)
  blocking collectives  40.5 us (14%)
  local copies, waits for them, and re-layouts  31.9 us (11%)
  matrix products  20.3 us (7%)
  between operations  14.1 us (5%)
  other arithmetic  8.33 us (3%)
    all_to_all x1, starting transfers between devices, local(): lax.all_to_all(normed, 'seq', split_axis=1, concat_axis=0, tiled=True)  46.7 us
    ppermute x2, waiting for transfers between devices, gather_around(): lax.ppermute(going_up, axis, [(d, (d + 1) % ways) for d in range(ways)])  45 us
    all_to_all x1, waiting for transfers between devices, local(): lax.all_to_all(normed, 'seq', split_axis=1, concat_axis=0, tiled=True)  34.7 us
    all_gather x2, blocking collectives, combined_all(): gathered = jax.tree.map(lambda a: lax.all_gather(a, axis), part)  28.2 us
    reduce_scatter x1, waiting for transfers between devices, local(): lax.psum_scatter(kv_full, 'tensor', scatter_dimension=2, tiled=True)  16.1 us
    all_gather x1, blocking collectives, local(): query_all = lax.all_gather(queries_grouped, 'seq', axis=0, tiled=True)  12.3 us
    reduce_scatter x1, waiting for transfers between devices, local(): lax.psum_scatter(jnp.dot(rows, out_weight, preferred_element_type=jnp.flo...  9.52 us
    dot_general x1, matrix products, local(): jnp.einsum('vd,jdc->jvc', vision_states, gather_around(key_value_weight,...  7.24 us
  transfers between devices with their start and end apart: 9, of which 6 were waited for; matrix products, arithmetic and copies ran while one was open for 16% of the time, Pallas kernels for 0%

profile of v1, /device:TPU:0, one launch (start us, length us, event | category | flops | bytes accessed | tf_op | source)
XLA Modules:
  0.0 283.6 jit_solution(15184674129778385231)
XLA Ops:
  6.5 3.0 %collective-permute-start = (bf16[2,2048,256]{2,1,0:T(8,128)(2,1)}, bf16[2,2048,256]{2,1,0:T(8,128)(2,1)}, u32[]{:S(2)}, u32[]{:S(2)}) collective-permute-start(bf16[2,2048,256]{2,1,0:T(8,128)(2,1)} %param.17), channel_id=1, source_target_pairs={{0,4},{4,8},{8,12},{12,0},{1,5},{5,9},{9,13},{13,1},{2,6},{6,10},{... | collective-permute-start | bytes 6291464 | tf_op jit(solution)/shard_map/ppermute | solution.py:20
  9.6 2.0 collective-permute-start.1
  11.6 0.7 convert_element_type.43
  12.3 1.1 fusion.9
  13.4 45.0 %collective-permute-done = bf16[2,2048,256]{2,1,0:T(8,128)(2,1)} collective-permute-done((bf16[2,2048,256]{2,1,0:T(8,128)(2,1)}, bf16[2,2048,256]{2,1,0:T(8,128)(2,1)}, u32[]{:S(2)}, u32[]{:S(2)}) %collective-permute-start) | collective-permute-done | bytes 2097184 | tf_op jit(solution)/shard_map/ppermute | solution.py:20
  58.4 1.6 fusion.11
  60.1 46.7 %all-to-all-start.1 = ((bf16[8,4,2048]{2,0,1:T(8,128)(2,1)}), bf16[8,4,2048]{2,0,1:T(8,128)(2,1)S(1)}, u32[]{:S(2)}, u32[]{:S(2)}) async-start(bf16[8,4,2048]{2,0,1:T(8,128)(2,1)} %bitcast.14), calls=%async_computation.2 | async-start | bytes 262144 | tf_op jit(solution)/shard_map/all_to_all | solution.py:114
  106.7 2.9 %copy.102 = bf16[2,2048,256]{1,2,0:T(8,128)(2,1)S(1)} copy(bf16[2,2048,256]{2,1,0:T(8,128)(2,1)} %param.17) | data formatting | bytes 4194304 | tf_op args[4]
  109.7 4.3 %broadcast_in_dim.56 = bf16[2,2048,1024]{1,2,0:T(8,128)(2,1)} broadcast(bf16[]{:T(256)} %constant.146.clone.1), dimensions={} | broadcast | bytes 8388610 | tf_op jit(solution)/shard_map/broadcast_in_dim | solution.py:16
  114.0 1.4 constant_dynamic-update-slice_fusion.3
  115.4 34.7 %all-to-all-done.1 = bf16[8,4,2048]{2,0,1:T(8,128)(2,1)S(1)} async-done(((bf16[8,4,2048]{2,0,1:T(8,128)(2,1)}), bf16[8,4,2048]{2,0,1:T(8,128)(2,1)S(1)}, u32[]{:S(2)}, u32[]{:S(2)}) %all-to-all-start.1) | async-done | bytes 131104 | tf_op jit(solution)/shard_map/all_to_all | solution.py:114
  150.1 5.6 %fusion.20 = f32[32,2048]{1,0:T(8,128)} fusion(bf16[2048,2048]{1,0:T(8,128)(2,1)} %param.16, bf16[8,4,2048]{2,0,1:T(8,128)(2,1)S(1)} %all-to-all-done.1), kind=kOutput, calls=%fused_computation.36 | convolution fusion | flops 268435456 | bytes 8781824 | tf_op jit(solution)/shard_map/dot_general | solution.py:118
  155.8 2.9 %copy.103 = bf16[2,2048,256]{1,2,0:T(8,128)(2,1)S(1)} copy(bf16[2,2048,256]{2,1,0:T(8,128)(2,1)} %collective-permute-done) | data formatting | bytes 4194304 | tf_op jit(solution)/shard_map/ppermute | solution.py:20
  158.8 4.0 %copy.104 = bf16[2,2048,256]{1,2,0:T(8,128)(2,1)} copy(bf16[2,2048,256]{2,1,0:T(8,128)(2,1)} %collective-permute-done.1) | data formatting | bytes 4194304 | tf_op jit(solution)/shard_map/ppermute | solution.py:23
  162.8 1.4 constant_dynamic-update-slice_fusion.2
  164.2 3.2 %constant_dynamic-update-slice_fusion.1 = bf16[2,2048,1024]{1,2,0:T(8,128)(2,1)} fusion(bf16[2,2048,1024]{1,2,0:T(8,128)(2,1)} %constant_dynamic-update-slice_fusion.2, bf16[2,2048,256]{1,2,0:T(8,128)(2,1)} %copy.104, s32[]{:T(128)S(6)} %select_n.107), kind=kLoop, calls=%fused_computation.58 | loop fusion | bytes 4194308 | tf_op jit(solution)/shard_map/dynamic_update_slice | solution.py:24
  167.4 2.9 %copy.105 = bf16[2,2048,256]{1,2,0:T(8,128)(2,1)S(1)} copy(bf16[2,2048,256]{2,1,0:T(8,128)(2,1)} %collective-permute-done.2) | data formatting | bytes 4194304 | tf_op jit(solution)/shard_map/ppermute | solution.py:20
  170.3 1.5 constant_dynamic-update-slice_fusion
  171.8 7.2 %convolution_bitcast_fusion = f32[2,256,1024]{1,2,0:T(8,128)} fusion(bf16[2,2048,1024]{1,2,0:T(8,128)(2,1)} %constant_dynamic-update-slice_fusion, bf16[256,2048]{1,0:T(8,128)(2,1)S(1)} %copy-done), kind=kOutput, calls=%fused_computation.10 | convolution fusion | flops 2147483648 | bytes 11534336 | tf_op jit(solution)/shard_map/vd,jdc->jvc/dot_general | solution.py:126
  179.2 0.1 select_reduce_fusion
  179.3 0.2 fusion.6
  179.5 0.9 bitcast_reduce_fusion
  180.5 0.1 copy.107
  180.5 0.1 copy.123
  180.6 0.9 multiply_convert_fusion.1
  181.5 12.3 %all_gather.21 = bf16[32,2,8,128]{3,0,2,1:T(8,128)(2,1)S(1)} all-gather(bf16[8,2,8,128]{3,0,2,1:T(8,128)(2,1)S(1)} %multiply_convert_fusion.1), channel_id=1, replica_groups=mesh['groups'=2,'seq'=4,'tensor'=4] {'seq'}, dimensions={0}, use_global_device_ids=true | all-gather | bytes 163840 | tf_op jit(solution)/shard_map/all_gather | solution.py:140
  193.8 16.1 %reduce-scatter.4.cloned.1.call-done = f32[2,256,256]{1,2,0:T(8,128)} async-done(((f32[2,256,1024]{1,2,0:T(8,128)}), f32[2,256,256]{1,2,0:T(8,128)}) %reduce-scatter.4.cloned.1.call-update) | async-done | bytes 524304 | tf_op jit(solution)/shard_map/reduce_scatter | solution.py:132
  209.9 1.0 slice.15
  210.9 0.1 copy.106
  211.1 0.4 fusion.33
  211.5 1.0 slice.21
  212.5 1.2 convolution_bitcast_fusion.1
  213.7 0.1 copy.109
  213.8 0.3 fusion.8
  214.1 0.1 copy.110
  214.2 13.8 %all-gather.1 = f32[128,2,8]{2,1,0:T(2,128)S(1)} all-gather(f32[32,2,8]{2,1,0:T(2,128)S(1)} %copy.110), channel_id=3, replica_groups=mesh['groups'=2,'seq'=4,'tensor'=4] {'seq'}, dimensions={0}, use_global_device_ids=true | all-gather | bytes 10240 | tf_op jit(solution)/shard_map/all_gather | solution.py:31
  227.9 0.1 copy.115
  228.0 0.1 copy.118
  228.1 14.5 %all-gather = f32[128,2,8]{2,1,0:T(2,128)S(1)} all-gather(f32[32,2,8]{2,1,0:T(2,128)S(1)} %copy.109), channel_id=2, replica_groups=mesh['groups'=2,'seq'=4,'tensor'=4] {'seq'}, dimensions={0}, use_global_device_ids=true | all-gather | bytes 10240 | tf_op jit(solution)/shard_map/all_gather | solution.py:31
  242.6 0.1 copy.114
  242.6 0.1 copy.117
  242.7 2.2 all-gather.5.cloned.1.call-done
  245.0 1.0 slice.19
  245.9 0.2 copy.116
  246.1 4.5 %while.19 = (s32[]{:T(128)}, f32[32,2,8]{0,2,1:T(8,128)S(1)}, f32[32,2,8]{0,2,1:T(8,128)S(1)}, f32[32,2,8,128]{3,2,1,0:T(8,128)S(1)}, f32[4,32,2,8]{1,3,2,0:T(8,...) while((s32[]{:T(128)}, f32[32,2,8]{0,2,1:T(8,128)S(1)}, ...), condition=%wide.region_9.10_spmd, body=%wide.region_8.9_spmd.sunk | while | flops 199685 | bytes 1339543 | solution.py:36
  246.1 0.1 copy.145
  246.2 0.1 copy.146
  246.3 1.0 constant_dynamic-slice_fusion.2
  247.3 0.3 fusion.42
  247.7 0.1 copy.145
  247.7 0.1 copy.146
  247.8 1.0 constant_dynamic-slice_fusion.2
  248.8 0.3 fusion.42
  249.2 0.1 copy.145
  249.3 0.1 copy.146
  249.3 1.0 constant_dynamic-slice_fusion.2
  250.3 0.3 fusion.42
  250.6 0.1 copy.120
  250.7 0.1 divide_convert_fusion
  250.9 5.6 %fusion.17 = f32[32,2048]{1,0:T(8,128)} fusion(bf16[2048,2048]{1,0:T(8,128)(2,1)} %param.18, bf16[4,8,16,128]{3,2,1,0:T(8,128)(2,1)S(1)} %bitcast.80), kind=kOutput, calls=%fused_computation.33 | convolution fusion | flops 268435456 | bytes 8781824 | tf_op jit(solution)/shard_map/dot_general | solution.py:150
  256.5 3.3 %all-to-all-start = ((bf16[8,4,2048]{2,0,1:T(8,128)(2,1)}), bf16[8,4,2048]{2,0,1:T(8,128)(2,1)S(1)}, u32[]{:S(2)}, u32[]{:S(2)}) async-start(bf16[8,4,2048]{2,0,1:T(8,128)(2,1)} %bitcast.3), calls=%async_computation | async-start | bytes 262144 | tf_op jit(solution)/shard_map/all_to_all | solution.py:113
  260.6 5.5 %all-to-all-done = bf16[8,4,2048]{2,0,1:T(8,128)(2,1)S(1)} async-done(((bf16[8,4,2048]{2,0,1:T(8,128)(2,1)}), bf16[8,4,2048]{2,0,1:T(8,128)(2,1)S(1)}, u32[]{:S(2)}, u32[]{:S(2)}) %all-to-all-start) | async-done | bytes 131104 | tf_op jit(solution)/shard_map/all_to_all | solution.py:113
  266.1 9.5 %reduce-scatter.8.cloned.1.call-done = f32[8,2048]{1,0:T(8,128)} async-done(((f32[32,2048]{1,0:T(8,128)}), f32[8,2048]{1,0:T(8,128)}) %reduce-scatter.8.cloned.1.call-update) | async-done | bytes 65552 | tf_op jit(solution)/shard_map/reduce_scatter | solution.py:149
  275.6 1.5 add_convert_fusion
  (35 shorter events, 0.4 us)
Async XLA Ops:
  6.5 165.3 %copy-start = (bf16[256,2048]{1,0:T(8,128)(2,1)S(1)}, bf16[256,2048]{1,0:T(8,128)(2,1)}, u32[]{:S(2)}) copy-start(bf16[256,2048]{1,0:T(8,128)(2,1)} %param.14) | copy-start | bytes 3145732
  6.5 51.9 %collective-permute-start = (bf16[2,2048,256]{2,1,0:T(8,128)(2,1)}, bf16[2,2048,256]{2,1,0:T(8,128)(2,1)}, u32[]{:S(2)}, u32[]{:S(2)}) collective-permute-start(bf16[2,2048,256]{2,1,0:T(8,128)(2,1)} %param.17), channel_id=1, source_target_pairs={{0,4},{4,8},{8,12},{12,0},{1,5},{5,9},{9,13},{13,1},{2,6},{6,10},{... | collective-permute-start | bytes 6291464 | tf_op jit(solution)/shard_map/ppermute | solution.py:20
  9.6 149.2 %collective-permute-start.1 = (bf16[2,2048,256]{2,1,0:T(8,128)(2,1)}, bf16[2,2048,256]{2,1,0:T(8,128)(2,1)}, u32[]{:S(2)}, u32[]{:S(2)}) collective-permute-start(bf16[2,2048,256]{2,1,0:T(8,128)(2,1)} %param.17), channel_id=1, source_target_pairs={{0,12},{4,0},{8,4},{12,8},{1,13},{5,1},{9,5},{13,9},{2,14},{6,2},{... | collective-permute-start | bytes 6291464 | tf_op jit(solution)/shard_map/ppermute | solution.py:23
  58.4 109.0 %collective-permute-start.2 = (bf16[2,2048,256]{2,1,0:T(8,128)(2,1)}, bf16[2,2048,256]{2,1,0:T(8,128)(2,1)}, u32[]{:S(2)}, u32[]{:S(2)}) collective-permute-start(bf16[2,2048,256]{2,1,0:T(8,128)(2,1)} %collective-permute-done), channel_id=1, source_target_pairs={{0,4},{4,8},{8,12},{12,0},{1,5},{5,9},{9,13},{13,1},{2,6},{6,10},{... | collective-permute-start | bytes 6291464 | tf_op jit(solution)/shard_map/ppermute | solution.py:20
  60.1 90.1 %all-to-all-start.1 = ((bf16[8,4,2048]{2,0,1:T(8,128)(2,1)}), bf16[8,4,2048]{2,0,1:T(8,128)(2,1)S(1)}, u32[]{:S(2)}, u32[]{:S(2)}) async-start(bf16[8,4,2048]{2,0,1:T(8,128)(2,1)} %bitcast.14), calls=%async_computation.2 | async-start | bytes 262144 | tf_op jit(solution)/shard_map/all_to_all | solution.py:114
  106.7 72.8 %reduce-scatter.6.cloned.1.call-start = ((), (), s32[]{:S(2)}) async-start(), calls=%async_computation.6 | async-start | bytes 327680 | tf_op jit(solution)/shard_map/reduce_scatter | solution.py:117
  155.8 54.1 %reduce-scatter.4.cloned.1.call-start = ((), (), s32[]{:S(2)}) async-start(), calls=%async_computation.5 | async-start | bytes 2621440 | tf_op jit(solution)/shard_map/reduce_scatter | solution.py:132
  171.8 7.4 %copy-start.3 = (s32[2]{0:T(128)S(1)}, s32[2]{0:T(128)}, u32[]{:S(2)}) copy-start(s32[2]{0:T(128)} %param.22) | copy-start | bytes 28
  171.8 7.5 %copy-start.4 = (s32[1,2]{1,0:T(1,128)S(1)}, s32[1,2]{1,0:T(1,128)}, u32[]{:S(2)}) copy-start(s32[1,2]{1,0:T(1,128)} %param.23) | copy-start | bytes 28
  171.8 8.8 %copy-start.1 = (f32[128]{0:T(128)S(1)}, f32[128]{0:T(128)}, u32[]{:S(2)}) copy-start(f32[128]{0:T(128)} %param.19) | copy-start | bytes 1540
  171.8 39.3 %copy-start.2 = (f32[128]{0:T(128)S(1)}, f32[128]{0:T(128)}, u32[]{:S(2)}) copy-start(f32[128]{0:T(128)} %param.20) | copy-start | bytes 1540
  179.1 65.9 %all-gather.5.cloned.1.call-start = ((), (), s32[]{:S(2)}) async-start(), calls=%async_computation.8 | async-start | bytes 1310720 | tf_op jit(solution)/shard_map/all_gather | solution.py:31
  213.7 61.9 %reduce-scatter.8.cloned.1.call-start = ((), (), s32[]{:S(2)}) async-start(), calls=%async_computation.7 | async-start | bytes 327680 | tf_op jit(solution)/shard_map/reduce_scatter | solution.py:149
  256.5 9.6 %all-to-all-start = ((bf16[8,4,2048]{2,0,1:T(8,128)(2,1)}), bf16[8,4,2048]{2,0,1:T(8,128)(2,1)S(1)}, u32[]{:S(2)}, u32[]{:S(2)}) async-start(bf16[8,4,2048]{2,0,1:T(8,128)(2,1)} %bitcast.3), calls=%async_computation | async-start | bytes 262144 | tf_op jit(solution)/shard_map/all_to_all | solution.py:113
Sparse Core Ops, SparseCore 0:
  155.9 18.9 reduce-scatter.5
  179.2 30.6 reduce-scatter.3
  213.8 31.1 all-gather.4
  256.6 18.9 reduce-scatter.7
